TPU v7x, 32 devices: a whole 2x2x4 slice. The times are simulated.
32 devices in a mesh: dp: 8 (over z, x), tp: 4 (over y, core).
Axes of the slice: x: 2, y: 2, z: 4, core: 2. Of those that a mesh axis runs over, the one named last changes fastest.
Arguments:
- tokens: bfloat16 [8192, 1024], P('dp'), may hold values from -6 to 6
- query_weight: bfloat16 [1024, 1024], P(None, 'tp'), may hold values from -0.1875 to 0.1875
- key_weight: bfloat16 [1024, 1024], P(None, 'tp'), may hold values from -0.1875 to 0.1875
- value_weight: bfloat16 [1024, 1024], P(None, 'tp'), may hold values from -0.1875 to 0.1875
- out_weight: bfloat16 [1024, 1024], P('tp'), may hold values from -0.75 to 0.75
- up_weight: bfloat16 [1024, 4096], P(None, 'tp'), may hold values from -0.1875 to 0.1875
- down_weight: bfloat16 [4096, 1024], P('tp'), may hold values from -0.09375 to 0.09375
- bias_table: float32 [32, 16], P(None, 'tp'), may hold values from -4 to 4
- gain_one: float32 [1024], replicated, may hold values from 0.5 to 1.5
- shift_one: float32 [1024], replicated, may hold values from -3 to 3
- gain_two: float32 [1024], replicated, may hold values from 0.5 to 1.5
- shift_two: float32 [1024], replicated, may hold values from -3 to 3
- single_item: int32 [8], P('dp'), may hold values 0 or 1
- cotangent: bfloat16 [8192, 1024], P('dp'), may hold values from -6 to 6
Outputs:
- result: bfloat16 [8192, 1024], P('dp')
- grad_tokens: float32 [8192, 1024], P('dp')
- grad_query_weight: float32 [1024, 1024], P(None, 'tp')
- grad_key_weight: float32 [1024, 1024], P(None, 'tp')
- grad_value_weight: float32 [1024, 1024], P(None, 'tp')
- grad_out_weight: float32 [1024, 1024], P('tp')
- grad_up_weight: float32 [1024, 4096], P(None, 'tp')
- grad_down_weight: float32 [4096, 1024], P('tp')
- grad_bias_table: float32 [32, 16], P(None, 'tp')
- grad_gain_one: float32 [1024], replicated
- grad_shift_one: float32 [1024], replicated
- grad_gain_two: float32 [1024], replicated
- grad_shift_two: float32 [1024], replicated
All inputs are finite; a program needn't handle non-finite values. No bound on the sum of `single_item` on one device may be relied on, other than what follows from the above.
Results may differ from a plain program's by a relative error of at most 0.023.
Values may be sent and summed in bfloat16 or wider, within the bound.
No kernel may reach another device: no remote copies, remote signals or barrier semaphores. Data moves between devices by JAX's collectives and lax.ppermute only.
A program may use at most 832 MiB of HBM per device.

v0:
```python
import math

import jax
import jax.numpy as jnp
from jax import lax
from jax.sharding import PartitionSpec as P

HD = 64
NB = 32
MAXDIST = 128


epsilon = 1e-05


def thresholds_list():
    exact_count = NB // 2
    thresholds = []
    for bucket in range(1, NB):
        if bucket <= exact_count:
            thresholds.append(bucket)
        else:
            thresholds.append(
                int(
                    math.ceil(
                        exact_count
                        * (MAXDIST / exact_count) ** ((bucket - exact_count) / exact_count)
                    )
                )
            )
    return thresholds


def distance_onehot(count):
    distance = jnp.arange(count, dtype=jnp.int32)
    buckets = jnp.zeros((count,), jnp.int32)
    for threshold in thresholds_list():
        buckets = buckets + (distance >= threshold).astype(jnp.int32)
    return (buckets[:, None] == jnp.arange(NB, dtype=jnp.int32)[None, :]).astype(jnp.float32)


def band_totals(grad_scores, band):
    head_count, row_count = (grad_scores.shape[0], grad_scores.shape[1])
    blocks = row_count // band
    tiled = grad_scores.reshape(head_count, blocks, band, blocks, band)
    own = jnp.einsum(
        "hcidv,cd->hiv", tiled, jnp.eye(blocks, dtype=jnp.float32), precision=lax.Precision.HIGHEST
    )
    before = jnp.einsum(
        "hcidv,cd->hiv",
        tiled,
        jnp.eye(blocks, k=-1, dtype=jnp.float32),
        precision=lax.Precision.HIGHEST,
    )
    joined = jnp.concatenate([before, own], axis=2).reshape(head_count, band * 2 * band)
    row_idx = jnp.arange(band, dtype=jnp.int32)[:, None, None]
    col_idx = jnp.arange(2 * band, dtype=jnp.int32)[None, :, None]
    dist_idx = jnp.arange(band, dtype=jnp.int32)[None, None, :]
    selector = (
        (band + row_idx - col_idx == dist_idx).astype(jnp.float32).reshape(band * 2 * band, band)
    )
    return jnp.dot(
        joined, selector, precision=lax.Precision.HIGHEST, preferred_element_type=jnp.float32
    )


def norm_parts(values, gain, shift):
    center = values - jnp.mean(values, axis=-1, keepdims=True)
    scaled = lax.rsqrt(jnp.mean(center * center, axis=-1, keepdims=True) + epsilon)
    normal = center * scaled
    return (normal, scaled, normal * gain + shift)


def norm_back(grad_out, normal, scaled, gain):
    grad_norm = grad_out * gain
    inner_mean = jnp.mean(grad_norm * normal, axis=-1, keepdims=True)
    return scaled * (grad_norm - jnp.mean(grad_norm, axis=-1, keepdims=True) - normal * inner_mean)


def gelu_pair(values):
    cdf_part = 0.5 * (1.0 + lax.erf(values * (1.0 / math.sqrt(2.0))))
    slope = cdf_part + values * jnp.exp(-0.5 * values * values) * (1.0 / math.sqrt(2.0 * math.pi))
    return (0.5 * values * (1.0 + lax.erf(values * (1.0 / math.sqrt(2.0)))), slope)


def scores_of(query_heads, key_heads, rel_bias, allowed, score_scale):
    scores = (
        jnp.einsum("qhd,khd->hqk", query_heads, key_heads, preferred_element_type=jnp.float32)
        * score_scale
    )
    return jnp.where(allowed[None], scores + rel_bias, -1000000000.0)


def shards(
    tokens,
    query_weight,
    key_weight,
    value_weight,
    out_weight,
    up_weight,
    down_weight,
    bias_table,
    gain_one,
    shift_one,
    gain_two,
    shift_two,
    single_item,
    cotangent,
):
    row_count = tokens.shape[0]
    head_count = bias_table.shape[1]
    band = min(MAXDIST, row_count)
    score_scale = HD ** (-0.5)
    head_shape = (row_count, head_count, HD)
    positions = jnp.arange(row_count, dtype=jnp.int32)
    segment = jnp.where(single_item[0] == 1, 0, (positions >= row_count // 2).astype(jnp.int32))
    allowed = (segment[:, None] == segment[None, :]) & (positions[None, :] <= positions[:, None])
    onehot = distance_onehot(band + 1)
    dist_bias = jnp.dot(
        onehot, bias_table, precision=lax.Precision.HIGHEST, preferred_element_type=jnp.float32
    ).T
    clipped = jnp.clip(positions[:, None] - positions[None, :], 0, band)
    rel_bias = jnp.take(dist_bias, clipped, axis=1)
    token_full = tokens.astype(jnp.float32)
    normal_one, scaled_one, normed = norm_parts(token_full, gain_one, shift_one)
    normed_low = normed.astype(jnp.bfloat16)
    queries = jnp.dot(normed_low, query_weight, preferred_element_type=jnp.float32).astype(
        jnp.bfloat16
    )
    key_rows = jnp.dot(normed_low, key_weight, preferred_element_type=jnp.float32).astype(
        jnp.bfloat16
    )
    value_rows = jnp.dot(normed_low, value_weight, preferred_element_type=jnp.float32).astype(
        jnp.bfloat16
    )
    query_heads = queries.reshape(head_shape)
    key_heads = key_rows.reshape(head_shape)
    value_heads = value_rows.reshape(head_shape)
    scores = scores_of(query_heads, key_heads, rel_bias, allowed, score_scale)
    row_max = jnp.max(scores, axis=-1, keepdims=True)
    exponent = jnp.exp(scores - row_max)
    row_total = jnp.sum(exponent, axis=-1, keepdims=True)
    log_total = row_max + jnp.log(row_total)
    probs_low = (exponent / row_total).astype(jnp.bfloat16)
    attended = jnp.einsum(
        "hqk,khd->qhd", probs_low, value_heads, preferred_element_type=jnp.float32
    )
    attended = attended.reshape(row_count, head_count * HD).astype(jnp.bfloat16)
    attn_sum = lax.psum(
        jnp.dot(attended, out_weight, preferred_element_type=jnp.float32).astype(jnp.bfloat16), "tp"
    ).astype(jnp.float32)
    residual = token_full + attn_sum
    normal_two, scaled_two, normed_two = norm_parts(residual, gain_two, shift_two)
    normed_two_low = normed_two.astype(jnp.bfloat16)
    inner_act = jnp.dot(normed_two_low, up_weight, preferred_element_type=jnp.float32)
    gelu_out, gelu_slope = gelu_pair(inner_act)
    active = gelu_out.astype(jnp.bfloat16)
    ffn_sum = lax.psum(
        jnp.dot(active, down_weight, preferred_element_type=jnp.float32).astype(jnp.bfloat16), "tp"
    ).astype(jnp.float32)
    result = (residual + ffn_sum).astype(jnp.bfloat16)
    grad_down = jnp.dot(active.T, cotangent, preferred_element_type=jnp.float32)
    grad_active = jnp.dot(cotangent, down_weight.T, preferred_element_type=jnp.float32)
    grad_inner = (grad_active * gelu_slope).astype(jnp.bfloat16)
    grad_up = jnp.dot(normed_two_low.T, grad_inner, preferred_element_type=jnp.float32)
    grad_normed_two = lax.psum(
        jnp.dot(grad_inner, up_weight.T, preferred_element_type=jnp.float32).astype(jnp.bfloat16),
        "tp",
    ).astype(jnp.float32)
    grad_gain_two = jnp.sum(grad_normed_two * normal_two, axis=0)
    grad_shift_two = jnp.sum(grad_normed_two, axis=0)
    grad_residual = cotangent.astype(jnp.float32) + norm_back(
        grad_normed_two, normal_two, scaled_two, gain_two
    )
    grad_residual_low = grad_residual.astype(jnp.bfloat16)
    grad_out = jnp.dot(attended.T, grad_residual_low, preferred_element_type=jnp.float32)
    grad_attended = jnp.dot(grad_residual_low, out_weight.T, preferred_element_type=jnp.float32)
    grad_attended = grad_attended.astype(jnp.bfloat16).reshape(head_shape)
    scores = scores_of(query_heads, key_heads, rel_bias, allowed, score_scale)
    probs_full = jnp.exp(scores - log_total)
    grad_value = jnp.einsum(
        "hqk,qhd->khd",
        probs_full.astype(jnp.bfloat16),
        grad_attended,
        preferred_element_type=jnp.float32,
    )
    grad_probs = jnp.einsum(
        "qhd,khd->hqk", grad_attended, value_heads, preferred_element_type=jnp.float32
    )
    row_dot = jnp.sum(probs_full * grad_probs, axis=-1, keepdims=True)
    grad_scores = probs_full * (grad_probs - row_dot)
    near_totals = band_totals(grad_scores, band)
    grad_table = jnp.dot(
        near_totals,
        onehot[:band],
        precision=lax.Precision.HIGHEST,
        preferred_element_type=jnp.float32,
    )
    far_total = jnp.sum(grad_scores, axis=(1, 2)) - jnp.sum(near_totals, axis=1)
    grad_table = grad_table + far_total[:, None] * onehot[band][None, :]
    grad_table = grad_table.T
    grad_scores_low = grad_scores.astype(jnp.bfloat16)
    grad_query = (
        jnp.einsum("hqk,khd->qhd", grad_scores_low, key_heads, preferred_element_type=jnp.float32)
        * score_scale
    )
    grad_key = (
        jnp.einsum("hqk,qhd->khd", grad_scores_low, query_heads, preferred_element_type=jnp.float32)
        * score_scale
    )
    grad_query = grad_query.astype(jnp.bfloat16).reshape(row_count, head_count * HD)
    grad_key = grad_key.astype(jnp.bfloat16).reshape(row_count, head_count * HD)
    grad_value = grad_value.astype(jnp.bfloat16).reshape(row_count, head_count * HD)
    grad_qw = jnp.dot(normed_low.T, grad_query, preferred_element_type=jnp.float32)
    grad_kw = jnp.dot(normed_low.T, grad_key, preferred_element_type=jnp.float32)
    grad_vw = jnp.dot(normed_low.T, grad_value, preferred_element_type=jnp.float32)
    grad_normed = jnp.dot(grad_query, query_weight.T, preferred_element_type=jnp.float32)
    grad_normed = grad_normed + jnp.dot(grad_key, key_weight.T, preferred_element_type=jnp.float32)
    grad_normed = grad_normed + jnp.dot(
        grad_value, value_weight.T, preferred_element_type=jnp.float32
    )
    grad_normed = lax.psum(grad_normed.astype(jnp.bfloat16), "tp").astype(jnp.float32)
    grad_gain_one = jnp.sum(grad_normed * normal_one, axis=0)
    grad_shift_one = jnp.sum(grad_normed, axis=0)
    grad_tokens = grad_residual + norm_back(grad_normed, normal_one, scaled_one, gain_one)
    summed = (
        lax.psum(grad_qw.astype(jnp.bfloat16), "dp").astype(jnp.float32),
        lax.psum(grad_kw.astype(jnp.bfloat16), "dp").astype(jnp.float32),
        lax.psum(grad_vw.astype(jnp.bfloat16), "dp").astype(jnp.float32),
        lax.psum(grad_out.astype(jnp.bfloat16), "dp").astype(jnp.float32),
        lax.psum(grad_up.astype(jnp.bfloat16), "dp").astype(jnp.float32),
        lax.psum(grad_down.astype(jnp.bfloat16), "dp").astype(jnp.float32),
        lax.psum(grad_table.astype(jnp.bfloat16), "dp").astype(jnp.float32),
        lax.psum(grad_gain_one.astype(jnp.bfloat16), "dp").astype(jnp.float32),
        lax.psum(grad_shift_one.astype(jnp.bfloat16), "dp").astype(jnp.float32),
        lax.psum(grad_gain_two.astype(jnp.bfloat16), "dp").astype(jnp.float32),
        lax.psum(grad_shift_two.astype(jnp.bfloat16), "dp").astype(jnp.float32),
    )
    return (
        result,
        grad_tokens,
        summed[0],
        summed[1],
        summed[2],
        summed[3],
        summed[4],
        summed[5],
        summed[6],
        summed[7],
        summed[8],
        summed[9],
        summed[10],
    )


def solution(mesh):
    placed = (
        P("dp", None),
        P(None, "tp"),
        P(None, "tp"),
        P(None, "tp"),
        P("tp", None),
        P(None, "tp"),
        P("tp", None),
        P(None, "tp"),
        P(),
        P(),
        P(),
        P(),
        P("dp"),
        P("dp", None),
    )
    return jax.shard_map(
        shards,
        mesh=mesh,
        in_specs=placed,
        out_specs=(
            P("dp", None),
            P("dp", None),
            P(None, "tp"),
            P(None, "tp"),
            P(None, "tp"),
            P("tp", None),
            P(None, "tp"),
            P("tp", None),
            P(None, "tp"),
            P(),
            P(),
            P(),
            P(),
        ),
        check_vma=False,
    )
```

profile of v0, /device:TPU:0, one launch (start us, length us, event | category | flops | bytes accessed | tf_op | source)
XLA Modules:
  0.0 4629.7 jit_solution(2698697681650478485)
XLA Ops:
  7.3 2.7 fusion.38
  12.0 3.2 copy.63
  17.8 3771.4 %gather_fusion = f32[1048576,4]{1,0:T(8,128)} fusion(f32[4,129]{0,1:T(8,128)S(1)} %copy.32, s32[1048576]{0:T(1024)} %broadcast_clamp_fusion), kind=kCustom, calls=%fused_computation | custom fusion | bytes 37748736 | tf_op jit(solution)/shard_map/jit(_take)/gather | solution.py:123
  3789.2 282.1 %copy.34 = f32[1024,1024,4]{0,1,2:T(8,128)} copy(f32[1024,1024,4]{2,1,0:T(8,128)} %bitcast.7) | data formatting | bytes 33554432 | tf_op jit(solution)/shard_map/jit(_take)/gather | solution.py:123
  4072.1 3.7 fusion.45
  4080.7 12.3 fusion.139
  4093.1 8.0 fusion.2
  4101.1 7.9 fusion.63
  4112.0 54.2 %all-reduce.8.cloned.1.call-done = bf16[1024,1024]{1,0:T(8,128)(2,1)} async-done(((bf16[1024,1024]{1,0:T(8,128)(2,1)}), bf16[1024,1024]{1,0:T(8,128)(2,1)}) %all-reduce.8.cloned.1.call-update) | async-done | bytes 2097168 | tf_op jit(solution)/shard_map/psum | solution.py:149
  4166.1 3.0 fusion.47
  4170.6 4.5 multiply_convert_fusion
  4175.1 3.6 fusion.37
  4180.0 3.8 convolution_convert_fusion.2
  4183.9 5.9 convolution_convert_fusion.3
  4189.7 45.7 all-reduce.10.cloned.1.call-done
  4235.4 5.7 fusion.29
  4241.1 3.4 fusion.27
  4247.4 14.1 multiply_reduce_fusion.2
  4264.0 13.4 fusion.138
  4277.3 7.4 fusion.60
  4284.8 8.6 fusion.57
  4293.4 3.0 fusion.54
  4301.6 6.1 convolution_convert_fusion
  4307.8 4.1 convolution_convert_fusion.1
  4319.0 14.4 copy.64
  4333.4 9.0 multiply_reduce_fusion.1
  4342.8 15.1 fusion.140
  4360.0 27.6 all-reduce.14.cloned.1.call-done
  4389.5 3.7 fusion.31
  4393.2 22.9 all-reduce
  4419.1 7.4 fusion.23
  4426.4 184.0 %all-reduce.12.cloned.1.call-done = (bf16[1024,256]{1,0:T(8,128)(2,1)}, bf16[1024,256]{1,0:T(8,128)(2,1)}, bf16[1024,256]{1,0:T(8,128)(2,1)}, bf16[256,1024]{1,0...) async-done(((bf16[1024,256]{1,0:T(8,128)(2,1)}, bf16[1024,256]{1,0:T(8,128)(2,1)}, bf16[1024,256]{1,0:T(8,128)(2,1)}, bf16[256,1024]{1,0:T(8,128)(2,1)}, ...) | async-done | bytes 6291472 | tf_op jit(solution)/shard_map/psum | solution.py:227
  (185 shorter events, 52.4 us)
Async XLA Ops:
  7.2 4163.3 %copy-start = (bf16[1024,1024]{1,0:T(8,128)(2,1)S(1)}, bf16[1024,1024]{1,0:T(8,128)(2,1)}, u32[]{:S(2)}) copy-start(bf16[1024,1024]{1,0:T(8,128)(2,1)} %param.19) | copy-start | bytes 6291460
  7.2 4158.9 %all-reduce.8.cloned.1.call-start = ((), (), s32[]{:S(2)}) async-start(), calls=%async_computation | async-start | bytes 4194304 | tf_op jit(solution)/shard_map/psum | solution.py:149
  3789.2 286.6 %copy-start.37 = (f32[1024]{0:T(1024)S(1)}, f32[1024]{0:T(1024)}, u32[]{:S(2)}) copy-start(f32[1024]{0:T(1024)} %copy-done.36) | copy-start | bytes 12292
  3789.2 286.6 %copy-start.39 = (f32[1024]{0:T(1024)S(1)}, f32[1024]{0:T(1024)}, u32[]{:S(2)}) copy-start(f32[1024]{0:T(1024)} %add_rsqrt_fusion.1) | copy-start | bytes 12292
  3789.2 286.6 %copy-start.41 = (f32[1024]{0:T(1024)S(1)}, f32[1024]{0:T(1024)}, u32[]{:S(2)}) copy-start(f32[1024]{0:T(1024)} %param.22) | copy-start | bytes 12292
  3789.2 286.6 %copy-start.46 = (f32[1024]{0:T(1024)S(1)}, f32[1024]{0:T(1024)}, u32[]{:S(2)}) copy-start(f32[1024]{0:T(1024)} %param.23) | copy-start | bytes 12292
  4071.3 7.0 copy-start.33
  4079.1 21.9 copy-start.29
  4079.9 13.1 copy-start.11
  4080.7 12.3 copy-start.13
  4101.0 8.7 copy-start.25
  4111.9 58.6 %copy-start.43 = (f32[1024]{0:T(1024)S(1)}, f32[1024]{0:T(1024)}, u32[]{:S(2)}) copy-start(f32[1024]{0:T(1024)} %param.24) | copy-start | bytes 12292
  4111.9 58.6 %copy-start.51 = (f32[1024]{0:T(1024)S(1)}, f32[1024]{0:T(1024)}, u32[]{:S(2)}) copy-start(f32[1024]{0:T(1024)} %param.25) | copy-start | bytes 12292
  4111.9 123.5 %all-reduce.10.cloned.1.call-start = ((), (), s32[]{:S(2)}) async-start(), calls=%async_computation.1 | async-start | bytes 4194304 | tf_op jit(solution)/shard_map/psum | solution.py:166
  4183.8 203.7 %all-reduce.14.cloned.1.call-start = ((), (), s32[]{:S(2)}) async-start(), calls=%async_computation.3 | async-start | bytes 8388608 | tf_op jit(solution)/shard_map/psum | solution.py:158
  4247.4 14.1 slice-start
  4247.4 14.1 slice-start.1
  4247.4 15.4 slice-start.2
  4247.4 16.6 slice-start.3
  4264.0 13.4 copy-start.14
  4277.3 7.5 copy-start.12
  4284.8 11.7 copy-start.19
  4301.5 6.2 copy-start.44
  4301.5 6.2 copy-start.52
  4301.5 308.9 %all-reduce.12.cloned.1.call-start = ((), (), s32[]{:S(2)}) async-start(), calls=%async_computation.2 | async-start | bytes 12582912 | tf_op jit(solution)/shard_map/psum | solution.py:227
  4342.4 15.4 copy-start.49
  4342.7 46.8 %copy-start.38 = (f32[1024]{0:T(1024)S(1)}, f32[1024]{0:T(1024)}, u32[]{:S(2)}) copy-start(f32[1024]{0:T(1024)} %copy-done.36) | copy-start | bytes 12292
  4342.7 46.8 %copy-start.40 = (f32[1024]{0:T(1024)S(1)}, f32[1024]{0:T(1024)}, u32[]{:S(2)}) copy-start(f32[1024]{0:T(1024)} %add_rsqrt_fusion.1) | copy-start | bytes 12292
  4342.8 46.8 %copy-start.42 = (f32[1024]{0:T(1024)S(1)}, f32[1024]{0:T(1024)}, u32[]{:S(2)}) copy-start(f32[1024]{0:T(1024)} %param.22) | copy-start | bytes 12292
  4357.9 35.3 copy-start.45
  4610.5 6.4 copy-start.35
  4610.5 7.5 copy-start.16
  (32 other events, 111.6 us)
Sparse Core Ops, SparseCore 0:
  4112.0 54.0 all-reduce.7
  4183.9 51.4 all-reduce.9
  4301.6 85.8 all-reduce.13
  4393.8 216.6 all-reduce.11
where the time goes:
time: 4710 us; the launch traced here: 4630 us
  local copies, waits for them, and re-layouts  4080 us (87%)
  waiting for transfers between devices  311 us (7%)
  matrix products  113 us (2%)
  other arithmetic  87.2 us (2%)
    gather x2, local copies, waits for them, and re-layouts, shards(): rel_bias = jnp.take(dist_bias, clipped, axis=1)  4050 us
    psum x1, waiting for transfers between devices, shards(): lax.psum(grad_qw.astype(jnp.bfloat16), 'dp').astype(jnp.float32)  184 us
  transfers between devices with their start and end apart: 4, of which 4 were waited for; matrix products, arithmetic and copies ran while one was open for 2% of the time, Pallas kernels for 0%

commit v1 on v0

--- a/solution.py
+++ b/solution.py
@@ -1,8 +1,11 @@
+import functools
 import math
 
 import jax
 import jax.numpy as jnp
 from jax import lax
+from jax.experimental import pallas as pl
+from jax.experimental.pallas import tpu as pltpu
 from jax.sharding import PartitionSpec as P
 
 HD = 64
@@ -39,31 +42,6 @@
     return (buckets[:, None] == jnp.arange(NB, dtype=jnp.int32)[None, :]).astype(jnp.float32)
 
 
-def band_totals(grad_scores, band):
-    head_count, row_count = (grad_scores.shape[0], grad_scores.shape[1])
-    blocks = row_count // band
-    tiled = grad_scores.reshape(head_count, blocks, band, blocks, band)
-    own = jnp.einsum(
-        "hcidv,cd->hiv", tiled, jnp.eye(blocks, dtype=jnp.float32), precision=lax.Precision.HIGHEST
-    )
-    before = jnp.einsum(
-        "hcidv,cd->hiv",
-        tiled,
-        jnp.eye(blocks, k=-1, dtype=jnp.float32),
-        precision=lax.Precision.HIGHEST,
-    )
-    joined = jnp.concatenate([before, own], axis=2).reshape(head_count, band * 2 * band)
-    row_idx = jnp.arange(band, dtype=jnp.int32)[:, None, None]
-    col_idx = jnp.arange(2 * band, dtype=jnp.int32)[None, :, None]
-    dist_idx = jnp.arange(band, dtype=jnp.int32)[None, None, :]
-    selector = (
-        (band + row_idx - col_idx == dist_idx).astype(jnp.float32).reshape(band * 2 * band, band)
-    )
-    return jnp.dot(
-        joined, selector, precision=lax.Precision.HIGHEST, preferred_element_type=jnp.float32
-    )
-
-
 def norm_parts(values, gain, shift):
     center = values - jnp.mean(values, axis=-1, keepdims=True)
     scaled = lax.rsqrt(jnp.mean(center * center, axis=-1, keepdims=True) + epsilon)
@@ -83,12 +61,216 @@
     return (0.5 * values * (1.0 + lax.erf(values * (1.0 / math.sqrt(2.0)))), slope)
 
 
-def scores_of(query_heads, key_heads, rel_bias, allowed, score_scale):
-    scores = (
-        jnp.einsum("qhd,khd->hqk", query_heads, key_heads, preferred_element_type=jnp.float32)
-        * score_scale
-    )
-    return jnp.where(allowed[None], scores + rel_bias, -1000000000.0)
+BLK = 256
+NEAR = 128
+NEG = -1000000000.0
+NT = (((1,), (1,)), ((), ()))
+TN = (((0,), (0,)), ((), ()))
+
+
+def dotf(a, b, dims=(((1,), (0,)), ((), ()))):
+    return lax.dot_general(a, b, dims, preferred_element_type=jnp.float32)
+
+
+def fill_bias(g_ref, bias_ref):
+    row = lax.broadcasted_iota(jnp.int32, (2 * NEAR, NEAR), 0)
+    col = lax.broadcasted_iota(jnp.int32, (2 * NEAR, NEAR), 1)
+    hidden = row - NEAR > col
+    for h in range(2):
+        spread = jnp.broadcast_to(g_ref[h : h + 1, :], (2 * NEAR, 2 * NEAR))
+        tile = pltpu.roll(spread, 0, 1, stride=1, stride_axis=0)[:, :NEAR]
+        tile = jnp.where(hidden, NEG, tile)
+        bias_ref[h, : 2 * NEAR, :NEAR] = tile
+        bias_ref[h, 2 * NEAR :, :NEAR] = jnp.full((NEAR, NEAR), NEG, jnp.float32)
+        bias_ref[h, :NEAR, NEAR:] = jnp.zeros((NEAR, NEAR), jnp.float32)
+        bias_ref[h, NEAR:, NEAR:] = tile
+
+
+def head_mask(x, h):
+    lane = lax.broadcasted_iota(jnp.int32, x.shape, 1)
+    return jnp.where((lane < HD) == (h == 0), x, jnp.zeros_like(x))
+
+
+def add_near(st, bias_ref, h, low, blk):
+    near = max(blk * BLK - NEAR, low)
+    top = near - low
+    tile = bias_ref[h, near - (blk * BLK - NEAR) :, :]
+    if top == 0:
+        return st + tile
+    return jnp.concatenate([st[:top], st[top:] + tile], axis=0)
+
+
+def each_block(row_count, single_ref, work):
+    half = row_count // 2
+    single = single_ref[0] == 1
+    for blk in range(row_count // BLK):
+        if blk * BLK < half:
+            work(blk, 0)
+        else:
+            pl.when(single)(functools.partial(work, blk, 0))
+            pl.when(jnp.logical_not(single))(functools.partial(work, blk, half))
+
+
+def attn_fwd_kernel(single_ref, g_ref, q_ref, k_ref, v_ref, o_ref, lse_ref, bias_ref, vt_ref):
+    row_count = q_ref.shape[0]
+    fill_bias(g_ref, bias_ref)
+    vt_ref[...] = v_ref[...].T
+
+    def work(blk, low):
+        high = (blk + 1) * BLK
+        rows = slice(blk * BLK, high)
+        q = q_ref[rows, :] * jnp.asarray(HD ** (-0.5), jnp.bfloat16)
+        outs = []
+        for h in range(2):
+            st = dotf(k_ref[low:high, :], head_mask(q, h), NT)
+            st = add_near(st, bias_ref, h, low, blk)
+            m = jnp.max(st, axis=0, keepdims=True)
+            p = jnp.exp(st - m)
+            total = jnp.sum(p, axis=0, keepdims=True)
+            ot = dotf(vt_ref[h * HD : (h + 1) * HD, low:high], p.astype(jnp.bfloat16))
+            outs.append(ot / total)
+            lse_ref[h : h + 1, rows] = m + jnp.log(total)
+        o_ref[rows, :] = jnp.concatenate(outs, axis=0).T.astype(jnp.bfloat16)
+
+    each_block(row_count, single_ref, work)
+
+
+def attn_bwd_kernel(
+    single_ref, g_ref, q_ref, k_ref, v_ref, o_ref, lse_ref, da_ref,
+    dq_ref, dk_ref, dv_ref, near_ref, bias_ref, kt_ref, dk_acc, dv_acc, near_acc,
+):
+    row_count = q_ref.shape[0]
+    fill_bias(g_ref, bias_ref)
+    kt_ref[...] = k_ref[...].T
+    dk_acc[...] = jnp.zeros_like(dk_acc)
+    dv_acc[...] = jnp.zeros_like(dv_acc)
+    near_acc[...] = jnp.zeros_like(near_acc)
+
+    def work(blk, low):
+        high = (blk + 1) * BLK
+        rows = slice(blk * BLK, high)
+        q = q_ref[rows, :] * jnp.asarray(HD ** (-0.5), jnp.bfloat16)
+        da = da_ref[rows, :]
+        prod_t = (da.astype(jnp.float32) * o_ref[rows, :].astype(jnp.float32)).T
+        ps, dss, qms, dams, dqts = [], [], [], [], []
+        for h in range(2):
+            qm, dam = head_mask(q, h), head_mask(da, h)
+            st = dotf(k_ref[low:high, :], qm, NT)
+            st = add_near(st, bias_ref, h, low, blk)
+            p = jnp.exp(st - lse_ref[h : h + 1, rows])
+            dpt = dotf(v_ref[low:high, :], dam, NT)
+            dd = jnp.sum(prod_t[h * HD : (h + 1) * HD], axis=0, keepdims=True)
+            ds = p * (dpt - dd)
+            own = blk * BLK - low
+            if own:
+                near_acc[h] += ds[own - NEAR : own + NEAR, :NEAR]
+            else:
+                near_acc[h, NEAR:] += ds[:NEAR, :NEAR]
+            near_acc[h] += ds[own : own + 2 * NEAR, NEAR:]
+            dsb = ds.astype(jnp.bfloat16)
+            ps.append(p.astype(jnp.bfloat16))
+            dss.append(dsb)
+            qms.append(qm)
+            dams.append(dam)
+            dqts.append(dotf(kt_ref[h * HD : (h + 1) * HD, low:high], dsb))
+        dv_acc[low:high] += dotf(jnp.concatenate(ps, axis=1), jnp.concatenate(dams, axis=0))
+        dk_acc[low:high] += dotf(jnp.concatenate(dss, axis=1), jnp.concatenate(qms, axis=0))
+        dq = jnp.concatenate(dqts, axis=0).T * HD ** (-0.5)
+        dq_ref[rows, :] = dq.astype(jnp.bfloat16)
+
+    each_block(row_count, single_ref, work)
+    dk_ref[...] = dk_acc[...].astype(jnp.bfloat16)
+    dv_ref[...] = dv_acc[...].astype(jnp.bfloat16)
+    near_ref[...] = jnp.zeros_like(near_ref)
+    for h in range(2):
+        acc = jnp.concatenate([near_acc[h], jnp.zeros((2 * NEAR, NEAR), jnp.float32)], axis=1)
+        row = lax.broadcasted_iota(jnp.int32, acc.shape, 0)
+        for bit in range((2 * NEAR - 1).bit_length()):
+            moved = pltpu.roll(acc, 2 * NEAR - (1 << bit), 1)
+            acc = jnp.where((row & (1 << bit)) != 0, moved, acc)
+        near_ref[h : h + 1, :] = jnp.sum(acc, axis=0, keepdims=True)
+
+
+def pair_specs(row_count):
+    smem = pl.BlockSpec(memory_space=pltpu.SMEM)
+    cols = pl.BlockSpec((row_count, 2 * HD), lambda p: (0, p))
+    near = pl.BlockSpec((None, 8, 2 * NEAR), lambda p: (p, 0, 0))
+    lse = pl.BlockSpec((None, 8, row_count), lambda p: (p, 0, 0))
+    return smem, cols, near, lse
+
+
+def attn_forward(single_item, g, q, k, v):
+    row_count, width = q.shape
+    pairs = width // (2 * HD)
+    smem, cols, near, lse = pair_specs(row_count)
+    return pl.pallas_call(
+        attn_fwd_kernel,
+        grid=(pairs,),
+        in_specs=[smem, near, cols, cols, cols],
+        out_specs=[cols, lse],
+        out_shape=[
+            jax.ShapeDtypeStruct((row_count, width), jnp.bfloat16),
+            jax.ShapeDtypeStruct((pairs, 8, row_count), jnp.float32),
+        ],
+        scratch_shapes=[
+            pltpu.VMEM((2, 3 * NEAR, BLK), jnp.float32),
+            pltpu.VMEM((2 * HD, row_count), jnp.bfloat16),
+        ],
+        compiler_params=pltpu.CompilerParams(vmem_limit_bytes=48 * 1024 * 1024),
+        cost_estimate=pl.CostEstimate(
+            flops=2 * row_count * row_count * width * 2,
+            bytes_accessed=8 * row_count * width,
+            transcendentals=row_count * row_count * width // HD // 2,
+        ),
+        name="attn_forward",
+    )(single_item, g, q, k, v)
+
+
+def attn_backward(single_item, g, q, k, v, o, lse_rows, da):
+    row_count, width = q.shape
+    pairs = width // (2 * HD)
+    smem, cols, near, lse = pair_specs(row_count)
+    flat = jax.ShapeDtypeStruct((row_count, width), jnp.bfloat16)
+    return pl.pallas_call(
+        attn_bwd_kernel,
+        grid=(pairs,),
+        in_specs=[smem, near, cols, cols, cols, cols, lse, cols],
+        out_specs=[cols, cols, cols, near],
+        out_shape=[flat, flat, flat, jax.ShapeDtypeStruct((pairs, 8, 2 * NEAR), jnp.float32)],
+        scratch_shapes=[
+            pltpu.VMEM((2, 3 * NEAR, BLK), jnp.float32),
+            pltpu.VMEM((2 * HD, row_count), jnp.bfloat16),
+            pltpu.VMEM((row_count, 2 * HD), jnp.float32),
+            pltpu.VMEM((row_count, 2 * HD), jnp.float32),
+            pltpu.VMEM((2, 2 * NEAR, NEAR), jnp.float32),
+        ],
+        compiler_params=pltpu.CompilerParams(vmem_limit_bytes=48 * 1024 * 1024),
+        cost_estimate=pl.CostEstimate(
+            flops=2 * row_count * row_count * width * 5,
+            bytes_accessed=16 * row_count * width,
+            transcendentals=row_count * row_count * width // HD // 2,
+        ),
+        name="attn_backward",
+    )(single_item, g, q, k, v, o, lse_rows, da)
+
+
+def near_bias(bias_table):
+    head_count = bias_table.shape[1]
+    rows = jnp.dot(
+        distance_onehot(NEAR), bias_table - bias_table[NB - 1 :],
+        precision=lax.Precision.HIGHEST, preferred_element_type=jnp.float32,
+    ).T
+    rows = jnp.pad(rows, ((0, 0), (NEAR, 0))).reshape(head_count // 2, 2, 2 * NEAR)
+    return jnp.pad(rows, ((0, 0), (0, 6), (0, 0)))
+
+
+def table_grad(near, head_count):
+    by_dist = near[:, :2, NEAR:].reshape(head_count, NEAR)
+    grad = jnp.dot(
+        by_dist, distance_onehot(NEAR)[:, : NB - 1],
+        precision=lax.Precision.HIGHEST, preferred_element_type=jnp.float32,
+    )
+    return jnp.concatenate([grad, -jnp.sum(grad, axis=1, keepdims=True)], axis=1).T
 
 
 def shards(
@@ -109,18 +291,7 @@
 ):
     row_count = tokens.shape[0]
     head_count = bias_table.shape[1]
-    band = min(MAXDIST, row_count)
-    score_scale = HD ** (-0.5)
-    head_shape = (row_count, head_count, HD)
-    positions = jnp.arange(row_count, dtype=jnp.int32)
-    segment = jnp.where(single_item[0] == 1, 0, (positions >= row_count // 2).astype(jnp.int32))
-    allowed = (segment[:, None] == segment[None, :]) & (positions[None, :] <= positions[:, None])
-    onehot = distance_onehot(band + 1)
-    dist_bias = jnp.dot(
-        onehot, bias_table, precision=lax.Precision.HIGHEST, preferred_element_type=jnp.float32
-    ).T
-    clipped = jnp.clip(positions[:, None] - positions[None, :], 0, band)
-    rel_bias = jnp.take(dist_bias, clipped, axis=1)
+    near_rows = near_bias(bias_table)
     token_full = tokens.astype(jnp.float32)
     normal_one, scaled_one, normed = norm_parts(token_full, gain_one, shift_one)
     normed_low = normed.astype(jnp.bfloat16)
@@ -133,19 +304,7 @@
     value_rows = jnp.dot(normed_low, value_weight, preferred_element_type=jnp.float32).astype(
         jnp.bfloat16
     )
-    query_heads = queries.reshape(head_shape)
-    key_heads = key_rows.reshape(head_shape)
-    value_heads = value_rows.reshape(head_shape)
-    scores = scores_of(query_heads, key_heads, rel_bias, allowed, score_scale)
-    row_max = jnp.max(scores, axis=-1, keepdims=True)
-    exponent = jnp.exp(scores - row_max)
-    row_total = jnp.sum(exponent, axis=-1, keepdims=True)
-    log_total = row_max + jnp.log(row_total)
-    probs_low = (exponent / row_total).astype(jnp.bfloat16)
-    attended = jnp.einsum(
-        "hqk,khd->qhd", probs_low, value_heads, preferred_element_type=jnp.float32
-    )
-    attended = attended.reshape(row_count, head_count * HD).astype(jnp.bfloat16)
+    attended, lse_rows = attn_forward(single_item, near_rows, queries, key_rows, value_rows)
     attn_sum = lax.psum(
         jnp.dot(attended, out_weight, preferred_element_type=jnp.float32).astype(jnp.bfloat16), "tp"
     ).astype(jnp.float32)
@@ -175,42 +334,11 @@
     grad_residual_low = grad_residual.astype(jnp.bfloat16)
     grad_out = jnp.dot(attended.T, grad_residual_low, preferred_element_type=jnp.float32)
     grad_attended = jnp.dot(grad_residual_low, out_weight.T, preferred_element_type=jnp.float32)
-    grad_attended = grad_attended.astype(jnp.bfloat16).reshape(head_shape)
-    scores = scores_of(query_heads, key_heads, rel_bias, allowed, score_scale)
-    probs_full = jnp.exp(scores - log_total)
-    grad_value = jnp.einsum(
-        "hqk,qhd->khd",
-        probs_full.astype(jnp.bfloat16),
-        grad_attended,
-        preferred_element_type=jnp.float32,
-    )
-    grad_probs = jnp.einsum(
-        "qhd,khd->hqk", grad_attended, value_heads, preferred_element_type=jnp.float32
-    )
-    row_dot = jnp.sum(probs_full * grad_probs, axis=-1, keepdims=True)
-    grad_scores = probs_full * (grad_probs - row_dot)
-    near_totals = band_totals(grad_scores, band)
-    grad_table = jnp.dot(
-        near_totals,
-        onehot[:band],
-        precision=lax.Precision.HIGHEST,
-        preferred_element_type=jnp.float32,
-    )
-    far_total = jnp.sum(grad_scores, axis=(1, 2)) - jnp.sum(near_totals, axis=1)
-    grad_table = grad_table + far_total[:, None] * onehot[band][None, :]
-    grad_table = grad_table.T
-    grad_scores_low = grad_scores.astype(jnp.bfloat16)
-    grad_query = (
-        jnp.einsum("hqk,khd->qhd", grad_scores_low, key_heads, preferred_element_type=jnp.float32)
-        * score_scale
-    )
-    grad_key = (
-        jnp.einsum("hqk,qhd->khd", grad_scores_low, query_heads, preferred_element_type=jnp.float32)
-        * score_scale
-    )
-    grad_query = grad_query.astype(jnp.bfloat16).reshape(row_count, head_count * HD)
-    grad_key = grad_key.astype(jnp.bfloat16).reshape(row_count, head_count * HD)
-    grad_value = grad_value.astype(jnp.bfloat16).reshape(row_count, head_count * HD)
+    grad_query, grad_key, grad_value, near_totals = attn_backward(
+        single_item, near_rows, queries, key_rows, value_rows, attended, lse_rows,
+        grad_attended.astype(jnp.bfloat16),
+    )
+    grad_table = table_grad(near_totals, head_count)
     grad_qw = jnp.dot(normed_low.T, grad_query, preferred_element_type=jnp.float32)
     grad_kw = jnp.dot(normed_low.T, grad_key, preferred_element_type=jnp.float32)
     grad_vw = jnp.dot(normed_low.T, grad_value, preferred_element_type=jnp.float32)

time: 4710 us -> 512 us (0.11); the launches traced: 4630 us -> 504 us
  local copies, waits for them, and re-layouts: 4080 us -> 6.78 us
  matrix products: 113 us -> 45.8 us
    gather x2 -> x0, local copies, waits for them, and re-layouts: 4050 us -> none  [shards(): rel_bias = jnp.take(dist_bias, clipped, axis=1)]
    dot_general x9 -> x2, matrix products: 68.8 us -> 0.46 us  [the longest x1 0.26 us: table_grad(): jnp.dot(by_dist, distance_onehot(NEAR)[:, :NB - 1], precision=lax.Precisi...]
  transfers between devices with their start and end apart: 4 -> 4, of which waited for: 4 -> 4; matrix products, arithmetic and copies ran while one was open for 2% -> 8% of each run, Pallas kernels for 0% -> 0%
where the time goes in v1:
time: 512 us; the launch traced here: 504 us
  waiting for transfers between devices  350 us (68%)
  matrix products  45.8 us (9%)
  other arithmetic  44.7 us (9%)
  blocking collectives  23.1 us (5%)
  Pallas kernels  17 us (3%)
  between operations  15.4 us (3%)
  local copies, waits for them, and re-layouts  6.78 us (1%)
    psum x1, waiting for transfers between devices, shards(): lax.psum(grad_qw.astype(jnp.bfloat16), 'dp').astype(jnp.float32)  185 us
    psum x1, waiting for transfers between devices, shards(): lax.psum(jnp.dot(active, down_weight, preferred_element_type=jnp.float32)...  66 us
    psum x1, waiting for transfers between devices, shards(): lax.psum(jnp.dot(attended, out_weight, preferred_element_type=jnp.float32...  54.1 us
    psum x1, waiting for transfers between devices, shards(): lax.psum(jnp.dot(grad_inner, up_weight.T, preferred_element_type=jnp.floa...  45.5 us
    psum x1, blocking collectives, shards(): lax.psum(grad_table.astype(jnp.bfloat16), 'dp').astype(jnp.float32)  23.1 us
  transfers between devices with their start and end apart: 4, of which 4 were waited for; matrix products, arithmetic and copies ran while one was open for 8% of the time, Pallas kernels for 0%

profile of v1, /device:TPU:0, one launch (start us, length us, event | category | flops | bytes accessed | tf_op | source)
XLA Modules:
  0.0 503.7 jit_solution(4481910500879371785)
XLA Ops:
  7.3 2.1 convert_reduce_fusion
  9.4 2.3 fusion.15
  13.3 1.5 convolution_convert_fusion.11.k_ref
  14.8 1.5 convolution_convert_fusion.12.q_ref
  19.6 7.2 %attn_forward.1 = (bf16[1024,256]{1,0:T(8,128)(2,1)S(1)}, f32[2,8,1024]{2,1,0:T(8,128)S(1)}) custom-call(s32[1]{0:T(128)S(6)} %copy.39.single_ref, f32[2,8,256]{2,1,0:T(8,128)S(1)} %pad.9.g_ref, bf16[1024,256]{1,0:T(8,128)(2,1)S(1)} %copy-done.4, bf16[1024,256]{1,0:T(8,128)(2,1)S(1)} %copy-done.2, bf16[1024,256]{1,0:T(8,128)(2,1)S(1)} %convolution_convert_fusion.10.v_ref), custom_call_target="tpu_custom_call" | custom-call | flops 1073741824 | bytes 2097152 | tf_op jit(solution)/shard_map/attn_forward/pallas_call | solution.py:206
  26.8 3.1 convolution_convert_fusion.4
  30.1 54.1 %all-reduce.10.cloned.1.call-done = bf16[1024,1024]{1,0:T(8,128)(2,1)} async-done(((bf16[1024,1024]{1,0:T(8,128)(2,1)}), bf16[1024,1024]{1,0:T(8,128)(2,1)}) %all-reduce.10.cloned.1.call-update) | async-done | bytes 2097168 | tf_op jit(solution)/shard_map/psum | solution.py:308
  84.2 3.0 fusion.29
  88.7 4.5 multiply_convert_fusion
  93.2 3.6 fusion.28
  98.1 3.8 convolution_convert_fusion.2
  102.0 6.0 %convolution_convert_fusion.3 = bf16[1024,1024]{1,0:T(8,128)(2,1)} fusion(bf16[1024,1024]{1,0:T(8,128)(2,1)} %get-tuple-element.48, bf16[1024,1024]{1,0:T(8,128)(2,1)} %param.20), kind=kOutput, calls=%fused_computation.48 | convolution fusion | flops 2148532224 | bytes 6291456 | tf_op jit(solution)/shard_map/dot_general | solution.py:318
  108.0 45.5 %all-reduce.12.cloned.1.call-done = bf16[1024,1024]{1,0:T(8,128)(2,1)} async-done(((bf16[1024,1024]{1,0:T(8,128)(2,1)}), bf16[1024,1024]{1,0:T(8,128)(2,1)}) %all-reduce.12.cloned.1.call-update) | async-done | bytes 2097168 | tf_op jit(solution)/shard_map/psum | solution.py:325
  153.5 4.6 fusion.20
  158.2 2.2 fusion.18
  162.5 9.8 %attn_backward.1 = (bf16[1024,256]{1,0:T(8,128)(2,1)S(1)}, bf16[1024,256]{1,0:T(8,128)(2,1)S(1)}, bf16[1024,256]{1,0:T(8,128)(2,1)S(1)}, f32[2,8,256]{2,1,0:T(8,128)S(1)}) custom-call(s32[1]{0:T(128)S(6)} %copy.39.single_ref, f32[2,8,256]{2,1,0:T(8,128)S(1)} %pad.9.g_ref, bf16[1024,256]{1,0:T(8,128)(2,1)S(1)} %copy-done.5, bf16[1024,256]{1,0:T(8,128)(2,1)S(1)} %copy-done.3, ...), custom_call_target="tpu_custom_call" | custom-call | flops 2684354560 | bytes 4194304 | tf_op jit(solution)/shard_map/attn_backward/pallas_call | solution.py:234
  174.1 2.1 add_convert_fusion
  176.5 6.1 %convolution_convert_fusion = bf16[1024,1024]{1,0:T(8,128)(2,1)} fusion(bf16[1024,1024]{1,0:T(8,128)(2,1)} %get-tuple-element.48, bf16[1024,1024]{1,0:T(8,128)(2,1)} %param.27), kind=kOutput, calls=%fused_computation.45 | convolution fusion | flops 2148532224 | bytes 6291456 | tf_op jit(solution)/shard_map/dot_general | solution.py:321
  182.7 4.1 convolution_convert_fusion.1
  186.8 1.6 convolution_convert_fusion.6
  188.3 1.6 convolution_convert_fusion.7
  189.9 1.6 convolution_convert_fusion.8
  192.3 1.5 convolution_convert_fusion.5
  194.4 2.1 reduce_sum.135
  196.6 66.0 %all-reduce.16.cloned.1.call-done = (bf16[1024,1024]{1,0:T(8,128)(2,1)}, bf16[1024,1024]{1,0:T(8,128)(2,1)}) async-done(((bf16[1024,1024]{1,0:T(8,128)(2,1)}, bf16[1024,1024]{1,0:T(8,128)(2,1)}), (bf16[1024,1024]{1,0:T(8,128)(2,1)}, bf16[1024,1024]{1,0:T(8,128)(2,1)})) %all-reduce.16.cloned.1.call-update) | async-done | bytes 4194320 | tf_op jit(solution)/shard_map/psum | solution.py:317
  262.6 2.0 reduce_sum.133
  264.5 3.6 fusion.22
  268.2 23.1 %all-reduce.2 = (bf16[32,4]{0,1:T(4,128)(2,1)S(1)}, bf16[1024]{0:T(1024)(128)(2,1)S(1)}, bf16[1024]{0:T(1024)(128)(2,1)S(1)}, bf16[1024]{0:T(1024)(128)(2,1)S(1)}, bf16[1024]{0:T(1024)(128)(2,1)S(1)}) all-reduce(bf16[32,4]{0,1:T(4,128)(2,1)S(1)} %maximum_bitcast_fusion, ...), channel_id=1, replica_groups=mesh['dp'=8,'tp'=4] {'dp'}, use_global_device_ids=true, to_apply=%region_19.20 | all-reduce | flops 4224 | bytes 16896 | tf_op jit(solution)/shard_map/psum | solution.py:361
  294.2 6.8 %fusion.14 = (f32[1024,1024]{1,0:T(8,128)}, bf16[1024,1024]{1,0:T(8,128)(2,1)}) fusion(f32[1024,1024]{1,0:T(8,128)} %copy-done.11, bf16[1024,1024]{1,0:T(8,128)(2,1)S(1)} %copy-done.10, bf16[1024,1024]{1,0:T(8,128)(2,1)} %get-tuple-element.43, f32[1024]{0:T(1024)S(1)} %broadcast_multiply_fusion, f32[1024]{0:T(1024)S(1)} %broadcast_multiply_fusion.1, ...), kind=kLoop, calls=%fused_computation.22 | loop fusion | flops 15728640 | bytes 18894848 | tf_op jit(solution)/shard_map/add | solution.py:353
  301.0 184.6 %all-reduce.14.cloned.1.call-done = (bf16[1024,256]{1,0:T(8,128)(2,1)}, bf16[1024,256]{1,0:T(8,128)(2,1)}, bf16[1024,256]{1,0:T(8,128)(2,1)}, bf16[256,1024]{1,0...) async-done(((bf16[1024,256]{1,0:T(8,128)(2,1)}, bf16[1024,256]{1,0:T(8,128)(2,1)}, bf16[1024,256]{1,0:T(8,128)(2,1)}, bf16[256,1024]{1,0:T(8,128)(2,1)}, ...) | async-done | bytes 6291472 | tf_op jit(solution)/shard_map/psum | solution.py:355
  485.6 4.2 convert_element_type.499
  489.8 2.6 convert_element_type.501
  (124 shorter events, 20.0 us)
Async XLA Ops:
  7.2 81.4 %copy-start = (bf16[1024,1024]{1,0:T(8,128)(2,1)S(1)}, bf16[1024,1024]{1,0:T(8,128)(2,1)}, u32[]{:S(2)}) copy-start(bf16[1024,1024]{1,0:T(8,128)(2,1)} %param.19) | copy-start | bytes 6291460
  7.2 4.5 copy-start.33
  7.2 4.5 copy-start.35
  7.2 77.0 %all-reduce.10.cloned.1.call-start = ((), (), s32[]{:S(2)}) async-start(), calls=%async_computation | async-start | bytes 4194304 | tf_op jit(solution)/shard_map/psum | solution.py:308
  7.3 4.5 copy-start.6
  7.3 5.3 %copy-start.27 = (bf16[1024,256]{1,0:T(8,128)(2,1)S(1)}, bf16[1024,256]{1,0:T(8,128)(2,1)}, u32[]{:S(2)}) copy-start(bf16[1024,256]{1,0:T(8,128)(2,1)} %param.17) | copy-start | bytes 1572868
  29.9 58.7 %copy-start.34 = (f32[1024]{0:T(1024)S(1)}, f32[1024]{0:T(1024)}, u32[]{:S(2)}) copy-start(f32[1024]{0:T(1024)} %param.24) | copy-start | bytes 12292
  29.9 58.7 %copy-start.38 = (f32[1024]{0:T(1024)S(1)}, f32[1024]{0:T(1024)}, u32[]{:S(2)}) copy-start(f32[1024]{0:T(1024)} %param.25) | copy-start | bytes 12292
  29.9 123.6 %all-reduce.12.cloned.1.call-start = ((), (), s32[]{:S(2)}) async-start(), calls=%async_computation.1 | async-start | bytes 4194304 | tf_op jit(solution)/shard_map/psum | solution.py:325
  84.2 3.0 copy-start.7
  84.2 3.5 copy-start.13
  88.6 4.5 copy-start.21
  88.6 4.5 copy-start.37
  101.9 160.6 %all-reduce.16.cloned.1.call-start = ((), (), s32[]{:S(2)}) async-start(), calls=%async_computation.3 | async-start | bytes 8388608 | tf_op jit(solution)/shard_map/psum | solution.py:317
  102.0 51.6 %copy-start.8 = (bf16[1024,1024]{1,0:T(8,128)(2,1)S(1)}, bf16[1024,1024]{1,0:T(8,128)(2,1)}, u32[]{:S(2)}) copy-start(bf16[1024,1024]{1,0:T(8,128)(2,1)} %param.14) | copy-start | bytes 6291460
  153.5 4.7 copy-start.14
  153.5 4.7 copy-start.16
  153.5 4.7 copy-start.22
  160.5 11.8 %copy-start.11 = (f32[1024,1024]{1,0:T(8,128)}, f32[1024,1024]{1,0:T(8,128)S(1)}, u32[]{:S(2)}) copy-start(f32[1024,1024]{1,0:T(8,128)S(1)} %fusion.18) | copy-start | bytes 12582916
  162.5 9.9 %copy-start.24 = (bf16[1024,256]{1,0:T(8,128)(2,1)S(1)}, bf16[1024,256]{1,0:T(8,128)(2,1)}, u32[]{:S(2)}) copy-start(bf16[1024,256]{1,0:T(8,128)(2,1)} %param.15) | copy-start | bytes 1572868
  176.2 309.4 %all-reduce.14.cloned.1.call-start = ((), (), s32[]{:S(2)}) async-start(), calls=%async_computation.2 | async-start | bytes 12582912 | tf_op jit(solution)/shard_map/psum | solution.py:355
  176.5 6.2 %copy-start.9 = (bf16[1024,1024]{1,0:T(8,128)(2,1)S(1)}, bf16[1024,1024]{1,0:T(8,128)(2,1)}, u32[]{:S(2)}) copy-start(bf16[1024,1024]{1,0:T(8,128)(2,1)} %param.14) | copy-start | bytes 6291460
  176.5 6.1 %copy-start.15 = (bf16[1024,1024]{1,0:T(8,128)(2,1)S(1)}, bf16[1024,1024]{1,0:T(8,128)(2,1)}, u32[]{:S(2)}) copy-start(bf16[1024,1024]{1,0:T(8,128)(2,1)} %all-reduce.10.cloned.1.call-done) | copy-start | bytes 6291460
  176.5 6.1 %copy-start.40 = (bf16[1024,1024]{1,0:T(8,128)(2,1)S(1)}, bf16[1024,1024]{1,0:T(8,128)(2,1)}, u32[]{:S(2)}) copy-start(bf16[1024,1024]{1,0:T(8,128)(2,1)} %copy-done.39) | copy-start | bytes 6291460
  182.7 4.1 copy-start.19
  194.4 99.8 %copy-start.10 = (bf16[1024,1024]{1,0:T(8,128)(2,1)S(1)}, bf16[1024,1024]{1,0:T(8,128)(2,1)}, u32[]{:S(2)}) copy-start(bf16[1024,1024]{1,0:T(8,128)(2,1)} %param.14) | copy-start | bytes 6291460
  485.6 4.2 copy-start.17
  489.8 2.6 copy-start.32
  489.8 3.7 copy-start.31
  489.8 4.7 copy-start.30
  489.8 5.8 %copy-start.29 = (bf16[256,1024]{1,0:T(8,128)(2,1)S(1)}, bf16[256,1024]{1,0:T(8,128)(2,1)}, u32[]{:S(2)}) copy-start(bf16[256,1024]{1,0:T(8,128)(2,1)} %get-tuple-element.39) | copy-start | bytes 1572868
  489.8 6.8 %copy-start.1 = (bf16[1024,1024]{1,0:T(8,128)(2,1)S(1)}, bf16[1024,1024]{1,0:T(8,128)(2,1)}, u32[]{:S(2)}) copy-start(bf16[1024,1024]{1,0:T(8,128)(2,1)} %param.19) | copy-start | bytes 6291460
  (13 other events, 21.2 us)
Sparse Core Ops, SparseCore 0:
  30.0 54.1 all-reduce.9
  102.0 51.4 all-reduce.11
  176.3 86.1 all-reduce.15
  268.8 216.7 all-reduce.13
